TPU v7x, 32 devices: a whole 2x2x4 slice. The times are simulated.
32 devices in a mesh: parts: 2 (over y), dp: 4 (over z), mp: 4 (over x, core).
Axes of the slice: x: 2, y: 2, z: 4, core: 2. Of those that a mesh axis runs over, the one named last changes fastest.
Arguments:
- tokens: bfloat16 [8192, 8192], P(('parts', 'dp'), 'mp'), parts along dimension 0, may hold values from -6 to 6
- input_norm_weight: bfloat16 [8192], P('mp'), may hold values from 0.25 to 1.75
- value_weight: bfloat16 [8192, 1024], P('mp'), may hold values from -0.09375 to 0.09375
- adapter_down_weight: bfloat16 [4, 8192, 64], P('dp', 'mp'), may hold values from -0.0625 to 0.0625
- adapter_up_weight: bfloat16 [4, 64, 1024], P('dp', None, 'mp'), may hold values from -0.75 to 0.75
- tile_owner_adapter: int32 [64], P(('parts', 'dp')), parts along dimension 0, may hold values from 0 to 3
- request_tile_count: int32 [8], P(('parts', 'dp')), parts along dimension 0, may hold values from 1 to 8
- adapter_storage_slot: int32 [4], replicated, may hold values from 0 to 3, each once
Outputs:
- values: bfloat16 [8192, 1024], P(('parts', 'dp'), 'mp'), parts along dimension 0
There are 2 independent parts, one for each index of `parts`. A program takes and returns all parts, laid end to end along the dimension named above; an argument that names none is the same for every part. Nothing has to cross between parts.
Inputs may be any that keep to these rules, and one draw needn't show every extreme that they name: Adapter a is stored at index adapter_storage_slot[a] of adapter_down_weight and adapter_up_weight; each slot holds one adapter.
All inputs are finite; a program needn't handle non-finite values.
Results may differ from a plain program's by a relative error of at most 0.012.
Values may be sent and summed in bfloat16 or wider, within the bound.
A program may use at most 64 MiB of HBM per device.

v0:
```python
import jax
import jax.numpy as jnp
from jax import lax
from jax.sharding import PartitionSpec as P

MODEL_WIDTH = 8192


def shards(
    tokens,
    input_norm_weight,
    value_weight,
    adapter_down_weight,
    adapter_up_weight,
    tile_owner_adapter,
    request_tile_count,
    adapter_storage_slot,
):
    count_rows = tokens.shape[0]
    local_feats = tokens.shape[1]
    tiles = count_rows // 128
    floats = tokens.astype(jnp.float32)
    squares = lax.psum(jnp.sum(floats * floats, axis=1), "mp")
    inv_rms = lax.rsqrt(squares / MODEL_WIDTH + 1e-05)
    normed = (floats * inv_rms[:, None] * input_norm_weight.astype(jnp.float32)[None, :]).astype(
        jnp.bfloat16
    )
    partial_sum = jnp.dot(normed, value_weight, preferred_element_type=jnp.float32)
    base = lax.psum_scatter(
        partial_sum.astype(jnp.bfloat16), "mp", scatter_dimension=1, tiled=True
    ).astype(jnp.float32)
    local_cols = base.shape[1]
    adapter_count = adapter_storage_slot.shape[0]
    compare = tile_owner_adapter[:, None] == jnp.arange(adapter_count, dtype=jnp.int32)[None, :]
    slot = jnp.sum(jnp.where(compare, adapter_storage_slot[None, :], 0), axis=1)
    tile_grouped = normed.reshape(tiles, 128, local_feats)
    all_down, all_up = (
        lax.all_gather(adapter_down_weight, "dp", axis=0, tiled=True),
        lax.all_gather(adapter_up_weight, "dp", axis=0, tiled=True),
    )
    select = (slot[:, None] == jnp.arange(all_down.shape[0], dtype=jnp.int32)[None, :]).astype(
        jnp.bfloat16
    )
    down_sel = jnp.einsum(
        "ts,sdr->tdr", select, all_down, preferred_element_type=jnp.float32
    ).astype(jnp.bfloat16)
    low_part = jnp.einsum(
        "tbd,tdr->tbr", tile_grouped, down_sel, preferred_element_type=jnp.float32
    )
    low = lax.psum(low_part.astype(jnp.bfloat16), "mp").astype(jnp.float32)
    up_sel = jnp.einsum("ts,srk->trk", select, all_up, preferred_element_type=jnp.float32)
    delta = jnp.einsum("tbr,trk->tbk", low, up_sel, precision=lax.Precision.HIGHEST)
    delta = 2.0 * delta.reshape(count_rows, local_cols)
    alive = jnp.arange(tiles, dtype=jnp.int32) < request_tile_count[0]
    alive_rows = jnp.repeat(alive, 128)
    return jnp.where(alive_rows[:, None], base + delta, 0.0).astype(jnp.bfloat16)


def solution(mesh):
    in_specs = (
        P(("parts", "dp"), "mp"),
        P("mp"),
        P("mp", None),
        P("dp", "mp", None),
        P("dp", None, "mp"),
        P(("parts", "dp")),
        P(("parts", "dp")),
        P(),
    )
    out_specs = P(("parts", "dp"), "mp")
    return jax.shard_map(shards, mesh=mesh, in_specs=in_specs, out_specs=out_specs, check_vma=False)
```

profile of v0, /device:TPU:0, one launch (start us, length us, event | category | flops | bytes accessed | tf_op | source)
XLA Modules:
  0.0 120.3 jit_solution(17744265190748466647)
XLA Ops:
  6.5 0.0 copy-start.2
  6.5 0.0 copy-start.1
  6.5 0.0 all-gather.2.cloned.1.call-start
  6.5 0.7 all-gather.2.cloned.1.call-update
  7.3 0.0 all-reduce.2.cloned.1.call-start
  7.3 0.7 convert_element_type.27
  8.0 3.1 %fusion = f32[1024]{0:T(1024)S(1)} fusion(bf16[1024,2048]{1,0:T(8,128)(2,1)} %param.8), kind=kLoop, calls=%fused_computation.2 | loop fusion | flops 6290432 | bytes 4198400 | tf_op jit(solution)/shard_map/reduce_sum | solution.py:23
  11.1 8.3 %psum.14 = f32[1024]{0:T(1024)S(1)} all-reduce(f32[1024]{0:T(1024)S(1)} %fusion), channel_id=1, replica_groups=mesh['parts'=2,'dp'=4,'mp'=4] {'mp'}, use_global_device_ids=true, to_apply=%region_1.0 | all-reduce | flops 1024 | bytes 8192 | tf_op jit(solution)/shard_map/psum | solution.py:23
  19.4 0.0 copy-done.2
  19.4 0.0 copy-done.1
  19.4 0.1 select_reduce_fusion
  19.5 5.1 %fusion.2 = bf16[1024,2048]{1,0:T(8,128)(2,1)} fusion(bf16[1024,2048]{1,0:T(8,128)(2,1)} %param.8, f32[2048]{0:T(1024)S(1)} %convert_element_type.27, f32[1024]{0:T(1024)S(1)} %add_rsqrt_fusion), kind=kLoop, calls=%fused_computation.4 | loop fusion | flops 8388608 | bytes 8400896 | tf_op jit(solution)/shard_map/convert_element_type | solution.py:25
  24.6 14.9 %all-gather.2.cloned.1.call-done = bf16[4,2048,64]{1,2,0:T(8,128)(2,1)} async-done(((bf16[1,2048,64]{1,2,0:T(8,128)(2,1)}), bf16[4,2048,64]{1,2,0:T(8,128)(2,1)}) %all-gather.2.cloned.1.call-update) | async-done | bytes 1048592 | tf_op jit(solution)/shard_map/all_gather | solution.py:38
  39.6 2.2 %convolution_convert_fusion = bf16[8,2048,64]{1,0,2:T(8,128)(2,1)S(1)} fusion(bf16[4,2048,64]{1,2,0:T(8,128)(2,1)} %all-gather.2.cloned.1.call-done, s32[8]{0:T(128)S(1)} %select_reduce_fusion), kind=kOutput, calls=%fused_computation.5 | convolution fusion | flops 9437216 | bytes 3145760 | tf_op jit(solution)/shard_map/ts,sdr->tdr/dot_general | solution.py:44
  41.8 4.6 %fusion.5 = bf16[8,128,64]{1,2,0:T(8,128)(2,1)} fusion(bf16[8,128,2048]{2,1,0:T(8,128)(2,1)} %bitcast.19, bf16[8,2048,64]{1,0,2:T(8,128)(2,1)S(1)} %convolution_convert_fusion), kind=kOutput, calls=%fused_computation.10 | convolution fusion | flops 268500992 | bytes 6422528 | tf_op jit(solution)/shard_map/tbd,tdr->tbr/dot_general | solution.py:47
  46.4 0.0 all-reduce.2.cloned.1.call-update
  46.4 0.0 copy-start
  46.5 0.0 reduce-scatter.2.cloned.1.call-start
  46.5 9.3 %convolution_convert_fusion.1 = bf16[1024,1024]{1,0:T(8,128)(2,1)} fusion(bf16[1024,2048]{1,0:T(8,128)(2,1)} %fusion.2, bf16[2048,1024]{1,0:T(8,128)(2,1)} %param.10), kind=kOutput, calls=%fused_computation.8 | convolution fusion | flops 4296015872 | bytes 10485760 | tf_op jit(solution)/shard_map/dot_general | solution.py:28
  55.8 0.0 reduce-scatter.2.cloned.1.call-update
  56.5 0.0 copy-done
  56.5 13.4 %all_gather.7 = bf16[4,64,256]{2,1,0:T(8,128)(2,1)S(1)} all-gather(bf16[1,64,256]{2,1,0:T(8,128)(2,1)S(1)} %copy-done), channel_id=1, replica_groups=mesh['parts'=2,'dp'=4,'mp'=4] {'dp'}, dimensions={0}, use_global_device_ids=true | all-gather | bytes 163840 | tf_op jit(solution)/shard_map/all_gather | solution.py:39
  69.9 0.1 broadcast_bitcast_fusion
  70.0 0.3 fusion.12
  70.3 7.2 %all-reduce.2.cloned.1.call-done = bf16[8,128,64]{1,2,0:T(8,128)(2,1)} async-done(((bf16[8,128,64]{1,2,0:T(8,128)(2,1)}), bf16[8,128,64]{1,2,0:T(8,128)(2,1)}) %all-reduce.2.cloned.1.call-update) | async-done | bytes 131088 | tf_op jit(solution)/shard_map/psum | solution.py:50
  77.5 1.6 %convolution_multiply_fusion = f32[8,128,256]{2,1,0:T(8,128)S(1)} fusion(bf16[8,128,64]{1,2,0:T(8,128)(2,1)} %all-reduce.2.cloned.1.call-done, f32[8,64,256]{2,0,1:T(8,128)S(1)} %fusion.12), kind=kOutput, calls=%fused_computation.9 | convolution fusion | flops 201588736 | bytes 1703936 | tf_op jit(solution)/shard_map/tbr,trk->tbk/dot_general | solution.py:52
  79.1 32.5 %reduce-scatter.2.cloned.1.call-done = bf16[1024,256]{1,0:T(8,128)(2,1)} async-done(((bf16[1024,1024]{1,0:T(8,128)(2,1)}), bf16[1024,256]{1,0:T(8,128)(2,1)}) %reduce-scatter.2.cloned.1.call-update) | async-done | bytes 524304 | tf_op jit(solution)/shard_map/reduce_scatter | solution.py:29
  111.6 2.2 %fusion.9 = bf16[1024,256]{1,0:T(8,128)(2,1)} fusion(f32[8,128,256]{2,1,0:T(8,128)S(1)} %convolution_multiply_fusion, bf16[1024,256]{1,0:T(8,128)(2,1)} %reduce-scatter.2.cloned.1.call-done, pred[1024]{0:T(1024)(128)(4,1)S(1)} %broadcast_bitcast_fusion), kind=kLoop, calls=%fused_computation.13 | loop fusion | flops 1048576 | bytes 2098176 | tf_op jit(solution)/shard_map/convert_element_type | solution.py:56
  (2 shorter events, 0.0 us)
Async XLA Ops:
  6.5 12.9 %copy-start.2 = (s32[8]{0:T(128)S(1)}, s32[8]{0:T(128)}, u32[]{:S(2)}) copy-start(s32[8]{0:T(128)} %param.13) | copy-start | bytes 100
  6.5 12.9 %copy-start.1 = (s32[4]{0:T(128)S(1)}, s32[4]{0:T(128)}, u32[]{:S(2)}) copy-start(s32[4]{0:T(128)} %param.15) | copy-start | bytes 52
  6.5 33.1 %all-gather.2.cloned.1.call-start = ((), (), s32[]{:S(2)}) async-start(), calls=%async_computation.2 | async-start | bytes 1310720 | tf_op jit(solution)/shard_map/all_gather | solution.py:38
  7.3 70.2 %all-reduce.2.cloned.1.call-start = ((), (), s32[]{:S(2)}) async-start(), calls=%async_computation.3 | async-start | bytes 262144 | tf_op jit(solution)/shard_map/psum | solution.py:50
  46.4 10.0 %copy-start = (bf16[1,64,256]{2,1,0:T(8,128)(2,1)S(1)}, bf16[1,64,256]{2,1,0:T(8,128)(2,1)}, u32[]{:S(2)}) copy-start(bf16[1,64,256]{2,1,0:T(8,128)(2,1)} %param.12) | copy-start | bytes 98308
  46.5 65.2 %reduce-scatter.2.cloned.1.call-start = ((), (), s32[]{:S(2)}) async-start(), calls=%async_computation.1 | async-start | bytes 2621440 | tf_op jit(solution)/shard_map/reduce_scatter | solution.py:29
Sparse Core Ops, SparseCore 0:
  8.9 30.6 all-gather.1
  46.6 30.8 all-reduce.1
  80.2 31.3 reduce-scatter.1
where the time goes:
time: 121 us; the launch traced here: 120 us
  waiting for transfers between devices  55.4 us (46%)
  blocking collectives  21.8 us (18%)
  matrix products  18 us (15%)
  between operations  13.8 us (11%)
  other arithmetic  11.1 us (9%)
    reduce_scatter x1, waiting for transfers between devices, shards(): lax.psum_scatter(partial_sum.astype(jnp.bfloat16), 'mp', scatter_dimensio...  32.5 us
    all_gather x1, waiting for transfers between devices, shards(): lax.all_gather(adapter_down_weight, 'dp', axis=0, tiled=True)  14.9 us
    all_gather x1, blocking collectives, shards(): lax.all_gather(adapter_up_weight, 'dp', axis=0, tiled=True)  13.4 us
    dot_general x1, matrix products, shards(): jnp.dot(normed, value_weight, preferred_element_type=jnp.float32)  9.29 us
    psum x1, blocking collectives, shards(): squares = lax.psum(jnp.sum(floats * floats, axis=1), 'mp')  8.35 us
    psum x1, waiting for transfers between devices, shards(): low = lax.psum(low_part.astype(jnp.bfloat16), 'mp').astype(jnp.float32)  7.19 us
    convert_element_type x1, other arithmetic, shards(): (floats * inv_rms[:, None] * input_norm_weight.astype(jnp.float32)[None,...  5.13 us
    dot_general x1, matrix products, shards(): jnp.einsum('tbd,tdr->tbr', tile_grouped, down_sel, preferred_element_type...  4.6 us
  transfers between devices with their start and end apart: 3, of which 3 were waited for; matrix products, arithmetic and copies ran while one was open for 17% of the time, Pallas kernels for 0%

commit v1 on v0

v1 whole, which is shorter than its diff:
```python
import functools

import jax
import jax.numpy as jnp
from jax import lax
from jax.experimental import pallas as pl
from jax.experimental.pallas import tpu as pltpu
from jax.sharding import PartitionSpec as P

TILE = 128
CORES = 2
MESH = pl.DeviceIdType.MESH
F32 = jnp.float32
BF16 = jnp.bfloat16


def kernel(
    sizes,
    owner_ref,
    count_ref,
    store_ref,
    tok_hbm,
    gain_ref,
    w_hbm,
    down_ref,
    up_ref,
    out_ref,
    tok,
    scaled,
    w,
    gath,
    pair_out,
    pair_in,
    acc,
    far_out,
    far_in,
    sq_cols,
    sq,
    low_sel,
    low_pack,
    low_pair,
    low_far_out,
    low_far_in,
    low_done,
    tok_sem,
    w_sem,
    pair_s,
    pair_r,
    far_s,
    far_r,
    sq_s,
    sq_r,
    up_s,
    dn_s,
    z_r,
    part_s,
    part_r,
    low_s,
    low_r,
    lowx_s,
    lowx_r,
):
    n_parts, n_dp, n_mp, chunk = sizes
    rows, feats = tok.shape
    block = w.shape[2]
    rank = down_ref.shape[1]
    lanes = 2 * rank
    xs = n_mp // CORES
    chunks = rows // chunk
    tiles = rows // TILE
    me_p, me_z, me = lax.axis_index("parts"), lax.axis_index("dp"), lax.axis_index("mp")
    x, c = me // CORES, me % CORES
    mate = x * CORES + (1 - c)

    def far_id(d):
        return lax.rem(x + d, xs) * CORES + c

    def col(d, core):
        return lax.rem(x + d, xs) * CORES + core

    def tok_copy(i):
        at = pl.ds(pl.multiple_of(i * chunk, chunk), chunk)
        return pltpu.make_async_copy(tok_hbm.at[at], tok.at[at], tok_sem.at[i])

    def w_copy(k, index):
        at = pl.ds(pl.multiple_of(index * block, block), block)
        return pltpu.make_async_copy(w_hbm.at[:, at], w.at[k], w_sem.at[k])

    order = list(range(1, xs)) + [0]
    w_list = []
    for d in order:
        for core in (1 - c, c):
            w_list.append((len(w_list), col(d, core)))
    tok_copy(0).start()
    w_copy(*w_list[0]).start()
    w_copy(*w_list[1]).start()
    for i in range(1, chunks):
        tok_copy(i).start()
    for item in w_list[2:]:
        w_copy(*item).start()

    barrier = pltpu.get_barrier_semaphore()
    has_up = me_z < n_dp - 1
    has_dn = me_z > 0
    for k in range(1, n_mp):
        pl.semaphore_signal(
            barrier, inc=1, device_id={"mp": lax.rem(me + k, n_mp)}, device_id_type=MESH
        )
    for k in range(1, n_parts):
        pl.semaphore_signal(
            barrier, inc=1, device_id={"parts": lax.rem(me_p + k, n_parts)}, device_id_type=MESH
        )

    @pl.when(has_up)
    def _():
        pl.semaphore_signal(barrier, inc=1, device_id={"dp": me_z + 1}, device_id_type=MESH)

    @pl.when(has_dn)
    def _():
        pl.semaphore_signal(barrier, inc=1, device_id={"dp": me_z - 1}, device_id_type=MESH)

    chain = has_up.astype(jnp.int32) + has_dn.astype(jnp.int32)
    pl.semaphore_wait(barrier, n_mp - 1 + n_parts - 1 + chain)

    own_rows = pl.ds(pl.multiple_of(me_z * rank, rank), rank)
    gath[own_rows, :feats] = down_ref[0]
    gath[own_rows, feats:] = up_ref[0]
    piece = rank // n_parts

    def part_of(a, p):
        return gath.at[pl.ds(pl.multiple_of(a * rank + p * piece, 16), piece)]

    def z_copy(a, to, sems):
        ref = part_of(a, me_p)
        return pltpu.make_async_remote_copy(
            ref, ref, sems.at[a], z_r.at[a], device_id={"dp": to}, device_id_type=MESH
        )

    def part_copy(a, k):
        ref = part_of(a, me_p)
        return pltpu.make_async_remote_copy(
            ref,
            ref,
            part_s.at[a, k],
            part_r.at[a, k],
            device_id={"parts": lax.rem(me_p + k, n_parts)},
            device_id_type=MESH,
        )

    @pl.when(has_up)
    def _():
        z_copy(me_z, me_z + 1, up_s).start()

    @pl.when(has_dn)
    def _():
        z_copy(me_z, me_z - 1, dn_s).start()

    def relay(k):
        below, above = me_z - k, me_z + k

        @pl.when(below >= 0)
        def _():
            z_copy(below, me_z, up_s).wait_recv()

            @pl.when(has_up)
            def _():
                z_copy(below, me_z + 1, up_s).start()

            for q in range(1, n_parts):
                part_copy(below, q).start()

        @pl.when(above < n_dp)
        def _():
            z_copy(above, me_z, dn_s).wait_recv()

            @pl.when(has_dn)
            def _():
                z_copy(above, me_z - 1, dn_s).start()

            for q in range(1, n_parts):
                part_copy(above, q).start()

    def pair_copy(d, i):
        at = pl.ds(pl.multiple_of(i * chunk, chunk), chunk)
        return pltpu.make_async_remote_copy(
            pair_out.at[d, at],
            pair_in.at[d, at],
            pair_s.at[d, i],
            pair_r.at[d, i],
            device_id={"mp": mate},
            device_id_type=MESH,
        )

    def far_copy(d, i):
        at = pl.ds(pl.multiple_of(i * chunk, chunk), chunk)
        return pltpu.make_async_remote_copy(
            far_out.at[d - 1, at],
            far_in.at[d - 1, at],
            far_s.at[d - 1, i],
            far_r.at[d - 1, i],
            device_id={"mp": far_id(d)},
            device_id_type=MESH,
        )

    def forward(d, i):
        at = pl.ds(pl.multiple_of(i * chunk, chunk), chunk)
        pair_copy(d, i).wait_recv()
        far_out[d - 1, at] = (acc[d, at] + pair_in[d, at].astype(F32)).astype(BF16)
        far_copy(d, i).start()

    for n, d in enumerate(order):
        for k in (0, 1):
            w_copy(*w_list[2 * n + k]).wait()

        def step(i, carry, n=n, d=d):
            at = pl.ds(pl.multiple_of(i * chunk, chunk), chunk)
            if n == 0:
                tok_copy(i).wait()
                scaled[at] = tok[at] * gain_ref[...]
            pair_out[d, at] = jnp.dot(
                scaled[at], w[2 * n], preferred_element_type=F32
            ).astype(BF16)
            pair_copy(d, i).start()
            acc[d, at] = jnp.dot(scaled[at], w[2 * n + 1], preferred_element_type=F32)
            if d > 0:

                @pl.when(i > 0)
                def _():
                    forward(d, i - 1)

            return carry

        lax.fori_loop(0, chunks, step, 0)
        if d > 0:
            forward(d, chunks - 1)
        if n == 0:
            relay(1)

            def squares(i, carry):
                at = pl.ds(pl.multiple_of(i * 32, 32), 32)
                t = tok[at].astype(F32)
                sq_cols[at] = jnp.broadcast_to(
                    jnp.sum(t * t, axis=1, keepdims=True), (32, TILE)
                )
                return carry

            lax.fori_loop(0, rows // 32, squares, 0)
            for t in range(tiles):
                sq[0, t : t + 1, :] = sq_cols[t * TILE : (t + 1) * TILE, :].T[0:1, :]
            for k in range(1, n_mp):
                sq_copy(sq, sq_s, sq_r, me, n_mp, k).start()
    for k in range(2, n_dp):
        relay(k)

    for a in range(n_dp):

        @pl.when(me_z != a)
        def _(a=a):
            for q in range(1, n_parts):
                other = lax.rem(me_p + n_parts - q, n_parts)
                ref = part_of(a, other)
                pltpu.make_async_remote_copy(
                    ref,
                    ref,
                    part_s.at[a, q],
                    part_r.at[a, q],
                    device_id={"parts": lax.rem(me_p + q, n_parts)},
                    device_id_type=MESH,
                ).wait_recv()

    lane = lax.broadcasted_iota(jnp.int32, (TILE, lanes), 1)
    upper = lane >= rank
    slots = [store_ref[owner_ref[t]] for t in range(tiles)]

    def low_step(t, carry):
        at = pl.ds(pl.multiple_of(t * TILE, TILE), TILE)
        slot = store_ref[owner_ref[t]]
        low = lax.dot_general(
            scaled[at], gath[:, :feats], (((1,), (1,)), ((), ())), preferred_element_type=F32
        )
        picked = jnp.zeros((TILE, lanes), F32)
        for g in range(n_dp // 2):
            picked = jnp.where(
                2 * g + upper.astype(jnp.int32) == slot,
                low[:, g * lanes : (g + 1) * lanes],
                picked,
            )
        low_sel[at] = picked + pltpu.roll(picked, rank, 1)
        return carry

    lax.fori_loop(0, tiles, low_step, 0)
    quarter = tiles // 4
    for h in range(CORES):
        for q in range(quarter):
            first = h * (tiles // 2) + q
            second = first + quarter
            low_pack[h, q * TILE : (q + 1) * TILE, :] = jnp.where(
                upper,
                low_sel[second * TILE : (second + 1) * TILE, :],
                low_sel[first * TILE : (first + 1) * TILE, :],
            ).astype(BF16)
    to_mate = pltpu.make_async_remote_copy(
        low_pack.at[1 - c],
        low_pair,
        low_s.at[0],
        low_r.at[0],
        device_id={"mp": mate},
        device_id_type=MESH,
    )
    to_mate.start()
    to_mate.wait_recv()
    low_far_out[...] = (low_pack[c].astype(F32) + low_pair[...].astype(F32)).astype(BF16)

    def low_far(d):
        return pltpu.make_async_remote_copy(
            low_far_out,
            low_far_in.at[d - 1],
            lowx_s.at[d - 1],
            lowx_r.at[d - 1],
            device_id={"mp": far_id(d)},
            device_id_type=MESH,
        )

    for d in range(1, xs):
        low_far(d).start()

    for i in range(chunks):
        at = pl.ds(i * chunk, chunk)
        pair_copy(0, i).wait_recv()
        acc[0, at] = acc[0, at] + pair_in[0, at].astype(F32)
    total = sq[0]
    for k in range(1, n_mp):
        sq_copy(sq, sq_s, sq_r, me, n_mp, k).wait_recv()
        total = total + sq[k]
    inv = lax.rsqrt(total / (feats * n_mp) + 1e-05)
    sq_cols[...] = jnp.concatenate(
        [jnp.broadcast_to(inv[t : t + 1, :], (TILE, TILE)).T for t in range(tiles)], axis=0
    )

    low_sum = low_far_out[...].astype(F32)
    for d in range(1, xs):
        low_far(d).wait_recv()
        low_sum = low_sum + low_far_in[d - 1].astype(F32)
    low_done[c] = low_sum.astype(BF16)
    done = pltpu.make_async_remote_copy(
        low_done.at[c],
        low_done.at[c],
        low_s.at[1],
        low_r.at[1],
        device_id={"mp": mate},
        device_id_type=MESH,
    )
    done.start()
    pltpu.make_async_remote_copy(
        low_done.at[1 - c],
        low_done.at[1 - c],
        low_s.at[1],
        low_r.at[1],
        device_id={"mp": mate},
        device_id_type=MESH,
    ).wait_recv()

    for t in range(tiles):
        at = slice(t * TILE, (t + 1) * TILE)
        h, j = t // (tiles // 2), t % (tiles // 2)
        q, second = j % quarter, j >= quarter
        packed = low_done[h, q * TILE : (q + 1) * TILE, :].astype(F32)
        rolled = pltpu.roll(packed, rank, 1)
        own = jnp.where(upper, packed, rolled) if second else jnp.where(upper, rolled, packed)
        spread = jnp.concatenate(
            [
                jnp.where(2 * g + upper.astype(jnp.int32) == slots[t], own, 0.0)
                for g in range(n_dp // 2)
            ],
            axis=1,
        ).astype(BF16)
        delta = jnp.dot(spread, gath[:, feats:], preferred_element_type=F32)
        acc[0, at] = acc[0, at] + 2.0 * delta

    for i in range(chunks):
        for d in range(1, xs):
            far_copy(d, i).wait_recv()
        for t in range(i * chunk // TILE, (i + 1) * chunk // TILE):
            at = slice(t * TILE, (t + 1) * TILE)
            value = acc[0, at]
            for d in range(1, xs):
                value = value + far_in[d - 1, at].astype(F32)
            scale = jnp.concatenate([sq_cols[at, :]] * (block // TILE), axis=1)
            out_ref[at, :] = jnp.where(t < count_ref[0], value * scale, 0.0).astype(BF16)

    for d in order:
        for i in range(chunks):
            pair_copy(d, i).wait_send()
            if d > 0:
                far_copy(d, i).wait_send()
    for k in range(1, n_mp):
        sq_copy(sq, sq_s, sq_r, me, n_mp, k).wait_send()
    to_mate.wait_send()
    done.wait_send()
    for d in range(1, xs):
        low_far(d).wait_send()
    for a in range(n_dp):

        @pl.when(jnp.logical_and(has_up, a <= me_z))
        def _(a=a):
            z_copy(a, me_z, up_s).wait_send()

        @pl.when(jnp.logical_and(has_dn, a >= me_z))
        def _(a=a):
            z_copy(a, me_z, dn_s).wait_send()

        @pl.when(me_z != a)
        def _(a=a):
            for q in range(1, n_parts):
                part_copy(a, q).wait_send()


def sq_copy(sq, sq_s, sq_r, me, n_mp, k):
    return pltpu.make_async_remote_copy(
        sq.at[0],
        sq.at[k],
        sq_s.at[k],
        sq_r.at[k],
        device_id={"mp": lax.rem(me + k, n_mp)},
        device_id_type=MESH,
    )


def shards(mesh, tokens, gain, weight, down, up, owner, count, store):
    n_parts, n_dp, n_mp = (mesh.shape[name] for name in ("parts", "dp", "mp"))
    rows, feats = tokens.shape
    cols = weight.shape[1]
    rank = down.shape[2]
    block = cols // n_mp
    xs = n_mp // CORES
    chunk = 256
    chunks = rows // chunk
    far = max(xs - 1, 1)
    low_rows = rows // 4
    vmem = pltpu.VMEM
    dma = pltpu.SemaphoreType.DMA
    smem = pl.BlockSpec(memory_space=pltpu.SMEM)
    in_vmem = pl.BlockSpec(memory_space=pltpu.VMEM)
    in_hbm = pl.BlockSpec(memory_space=pl.ANY)
    return pl.pallas_call(
        functools.partial(kernel, (n_parts, n_dp, n_mp, chunk)),
        out_shape=jax.ShapeDtypeStruct((rows, block), BF16),
        in_specs=[smem, smem, smem, in_hbm, in_vmem, in_hbm, in_vmem, in_vmem],
        out_specs=in_vmem,
        scratch_shapes=[
            vmem((rows, feats), BF16),
            vmem((rows, feats), BF16),
            vmem((n_mp, feats, block), BF16),
            vmem((n_dp * rank, feats + block), BF16),
            vmem((xs, rows, block), BF16),
            vmem((xs, rows, block), BF16),
            vmem((xs, rows, block), F32),
            vmem((far, rows, block), BF16),
            vmem((far, rows, block), BF16),
            vmem((rows, TILE), F32),
            vmem((n_mp, rows // TILE, TILE), F32),
            vmem((rows, 2 * rank), F32),
            vmem((CORES, low_rows, 2 * rank), BF16),
            vmem((low_rows, 2 * rank), BF16),
            vmem((low_rows, 2 * rank), BF16),
            vmem((far, low_rows, 2 * rank), BF16),
            vmem((CORES, low_rows, 2 * rank), BF16),
            dma((chunks,)),
            dma((n_mp,)),
            dma((xs, chunks)),
            dma((xs, chunks)),
            dma((far, chunks)),
            dma((far, chunks)),
            dma((n_mp,)),
            dma((n_mp,)),
            dma((n_dp,)),
            dma((n_dp,)),
            dma((n_dp,)),
            dma((n_dp, n_parts)),
            dma((n_dp, n_parts)),
            dma((2,)),
            dma((2,)),
            dma((far,)),
            dma((far,)),
        ],
        compiler_params=pltpu.CompilerParams(
            collective_id=0, has_side_effects=True, vmem_limit_bytes=56 * 1024 * 1024
        ),
    )(owner, count, store, tokens, gain.reshape(1, feats), weight, down.transpose(0, 2, 1), up)


def solution(mesh):
    in_specs = (
        P(("parts", "dp"), "mp"),
        P("mp"),
        P("mp", None),
        P("dp", "mp", None),
        P("dp", None, "mp"),
        P(("parts", "dp")),
        P(("parts", "dp")),
        P(),
    )
    out_specs = P(("parts", "dp"), "mp")
    return jax.shard_map(
        functools.partial(shards, mesh),
        mesh=mesh,
        in_specs=in_specs,
        out_specs=out_specs,
        check_vma=False,
    )
```

time: 121 us -> 46.7 us (0.39)
  waiting for transfers between devices: 55.4 us -> 0 us
  Pallas kernels: 0 us -> 42.7 us
  blocking collectives: 21.8 us -> 0 us
  matrix products: 18 us -> 0 us
  between operations: 13.8 us -> 0.66 us
  other arithmetic: 11.1 us -> 0 us
  local copies, waits for them, and re-layouts: 0.09 us -> 3.16 us
    pallas_call x0 -> x1, Pallas kernels: none -> 42.7 us  [shards(): pl.pallas_call(functools.partial(kernel, (n_parts, n_dp, n_mp, chunk)), o...]
    reduce_scatter x1 -> x0, waiting for transfers between devices: 32.5 us -> none  [shards(): lax.psum_scatter(partial_sum.astype(jnp.bfloat16), 'mp', scatter_dimensio...]
    dot_general x5 -> x0, matrix products: 18 us -> none  [the longest x1 9.29 us: shards(): jnp.dot(normed, value_weight, preferred_element_type=jnp.float32)]
    all_gather x1 -> x0, waiting for transfers between devices: 14.9 us -> none  [shards(): lax.all_gather(adapter_down_weight, 'dp', axis=0, tiled=True)]
    all_gather x1 -> x0, blocking collectives: 13.4 us -> none  [shards(): lax.all_gather(adapter_up_weight, 'dp', axis=0, tiled=True)]
    psum x1 -> x0, blocking collectives: 8.35 us -> none  [shards(): squares = lax.psum(jnp.sum(floats * floats, axis=1), 'mp')]
    convert_element_type x3 -> x0, other arithmetic: 7.97 us -> none  [the longest x1 5.13 us: shards(): (floats * inv_rms[:, None] * input_norm_weight.astype(jnp.float32)[None,...]
    psum x1 -> x0, waiting for transfers between devices: 7.19 us -> none  [shards(): low = lax.psum(low_part.astype(jnp.bfloat16), 'mp').astype(jnp.float32)]
  transfers between devices with their start and end apart: 3 -> 0, of which waited for: 3 -> 0; matrix products, arithmetic and copies ran while one was open for 17% -> 0% of each run, Pallas kernels for 0% -> 0%
where the time goes in v1:
time: 46.7 us; the launch traced here: 46.5 us
  Pallas kernels  42.7 us (91%)
  local copies, waits for them, and re-layouts  3.16 us (7%)
  between operations  0.66 us (1%)
    pallas_call x1, Pallas kernels, shards(): pl.pallas_call(functools.partial(kernel, (n_parts, n_dp, n_mp, chunk)), o...  42.7 us
    unnamed x1, local copies, waits for them, and re-layouts  1.87 us
    reshape x1, local copies, waits for them, and re-layouts, shards(): gain.reshape(1, feats)  1.29 us

profile of v1, /device:TPU:0, one launch (start us, length us, event | category | flops | bytes accessed | tf_op | source)
XLA Modules:
  0.0 46.5 jit_solution(8123717469455048004)
XLA Ops:
  0.7 1.3 %reshape.3.gain_ref = bf16[1,2048]{1,0:T(2,128)(2,1)} reshape(bf16[2048]{0:T(1024)(128)(2,1)} %param.9) | data formatting | bytes 8192 | tf_op jit(solution)/shard_map/reshape | solution.py:489
  1.9 42.7 %shard_map.82 = bf16[1024,256]{1,0:T(8,128)(2,1)} custom-call(s32[8]{0:T(128)} %owner_ref.1, s32[1]{0:T(128)S(6)} %copy.10.count_ref, s32[4]{0:T(128)} %store_ref.1, bf16[1024,2048]{1,0:T(8,128)(2,1)} %tok_hbm.1, bf16[1,2048]{1,0:T(2,128)(2,1)} %reshape.3.gain_ref, bf16[2048,1024]{1,0:T(8,128)(2,1)} %w_hbm.1, bf16[1,64,2048]{2,1,0:T(8,128)(2,1)} %bitcast.1, ...), custom_call_target="tpu_custom_call" | custom-call | tf_op jit(solution)/shard_map/pallas_call | solution.py:445
  44.6 1.9 %copy.11 = bf16[1024,256]{1,0:T(8,128)(2,1)} copy(bf16[1024,256]{1,0:T(8,128)(2,1)} %shard_map.82) | data formatting | bytes 1048576

commit v2 on v1

--- a/solution.py
+++ b/solution.py
@@ -208,49 +208,43 @@
         far_out[d - 1, at] = (acc[d, at] + pair_in[d, at].astype(F32)).astype(BF16)
         far_copy(d, i).start()
 
-    for n, d in enumerate(order):
-        for k in (0, 1):
-            w_copy(*w_list[2 * n + k]).wait()
-
-        def step(i, carry, n=n, d=d):
-            at = pl.ds(pl.multiple_of(i * chunk, chunk), chunk)
-            if n == 0:
-                tok_copy(i).wait()
-                scaled[at] = tok[at] * gain_ref[...]
-            pair_out[d, at] = jnp.dot(
-                scaled[at], w[2 * n], preferred_element_type=F32
-            ).astype(BF16)
-            pair_copy(d, i).start()
-            acc[d, at] = jnp.dot(scaled[at], w[2 * n + 1], preferred_element_type=F32)
-            if d > 0:
-
-                @pl.when(i > 0)
-                def _():
-                    forward(d, i - 1)
-
-            return carry
-
-        lax.fori_loop(0, chunks, step, 0)
-        if d > 0:
-            forward(d, chunks - 1)
+    def base_step(n, d, i):
+        at = pl.ds(i * chunk, chunk)
+        if i == 0:
+            w_copy(*w_list[2 * n]).wait()
         if n == 0:
-            relay(1)
-
-            def squares(i, carry):
-                at = pl.ds(pl.multiple_of(i * 32, 32), 32)
-                t = tok[at].astype(F32)
-                sq_cols[at] = jnp.broadcast_to(
-                    jnp.sum(t * t, axis=1, keepdims=True), (32, TILE)
-                )
-                return carry
-
-            lax.fori_loop(0, rows // 32, squares, 0)
-            for t in range(tiles):
-                sq[0, t : t + 1, :] = sq_cols[t * TILE : (t + 1) * TILE, :].T[0:1, :]
-            for k in range(1, n_mp):
-                sq_copy(sq, sq_s, sq_r, me, n_mp, k).start()
-    for k in range(2, n_dp):
-        relay(k)
+            tok_copy(i).wait()
+            scaled[at] = tok[at] * gain_ref[...].reshape(1, feats)
+        pair_out[d, at] = jnp.dot(scaled[at], w[2 * n], preferred_element_type=F32).astype(BF16)
+        pair_copy(d, i).start()
+        if i == 0:
+            w_copy(*w_list[2 * n + 1]).wait()
+        acc[d, at] = jnp.dot(scaled[at], w[2 * n + 1], preferred_element_type=F32)
+        if d > 0 and i > 0:
+            forward(d, i - 1)
+
+    for n, d in enumerate(order[:-1]):
+        for i in range(chunks):
+            base_step(n, d, i)
+            if n == 0 and i == chunks // 2:
+                relay(1)
+        forward(d, chunks - 1)
+
+    ones = jnp.ones((feats, TILE), BF16)
+    for i in range(chunks):
+        at = pl.ds(i * chunk, chunk)
+        sq_cols[at] = jnp.dot(tok[at] * tok[at], ones, preferred_element_type=F32)
+    for t in range(tiles):
+        sq[0, t : t + 1, :] = sq_cols[t * TILE : (t + 1) * TILE, :].T[0:1, :]
+    for k in range(1, n_mp):
+        sq_copy(sq, sq_s, sq_r, me, n_mp, k).start()
+    if n_dp > 2:
+        relay(2)
+    for i in range(chunks):
+        base_step(xs - 1, 0, i)
+        if i == chunks // 2 - 1:
+            for k in range(3, n_dp):
+                relay(k)
 
     for a in range(n_dp):
 
@@ -272,23 +266,25 @@
     upper = lane >= rank
     slots = [store_ref[owner_ref[t]] for t in range(tiles)]
 
-    def low_step(t, carry):
-        at = pl.ds(pl.multiple_of(t * TILE, TILE), TILE)
-        slot = store_ref[owner_ref[t]]
-        low = lax.dot_general(
-            scaled[at], gath[:, :feats], (((1,), (1,)), ((), ())), preferred_element_type=F32
-        )
-        picked = jnp.zeros((TILE, lanes), F32)
-        for g in range(n_dp // 2):
-            picked = jnp.where(
-                2 * g + upper.astype(jnp.int32) == slot,
-                low[:, g * lanes : (g + 1) * lanes],
-                picked,
-            )
-        low_sel[at] = picked + pltpu.roll(picked, rank, 1)
-        return carry
-
-    lax.fori_loop(0, tiles, low_step, 0)
+    for i in range(chunks):
+        low_all = lax.dot_general(
+            scaled[pl.ds(i * chunk, chunk)],
+            gath[:, :feats],
+            (((1,), (1,)), ((), ())),
+            preferred_element_type=F32,
+        )
+        for t in range(i * chunk // TILE, (i + 1) * chunk // TILE):
+            first = t * TILE - i * chunk
+            low = low_all[first : first + TILE]
+            picked = jnp.zeros((TILE, lanes), F32)
+            for g in range(n_dp // 2):
+                picked = jnp.where(
+                    2 * g + upper.astype(jnp.int32) == slots[t],
+                    low[:, g * lanes : (g + 1) * lanes],
+                    picked,
+                )
+            low_sel[t * TILE : (t + 1) * TILE] = picked + pltpu.roll(picked, rank, 1)
+
     quarter = tiles // 4
     for h in range(CORES):
         for q in range(quarter):
@@ -486,7 +482,7 @@
         compiler_params=pltpu.CompilerParams(
             collective_id=0, has_side_effects=True, vmem_limit_bytes=56 * 1024 * 1024
         ),
-    )(owner, count, store, tokens, gain.reshape(1, feats), weight, down.transpose(0, 2, 1), up)
+    )(owner, count, store, tokens, gain, weight, down.transpose(0, 2, 1), up)
 
 
 def solution(mesh):

time: 46.7 us -> 34.4 us (0.74)
  Pallas kernels: 42.7 us -> 31.7 us
  local copies, waits for them, and re-layouts: 3.16 us -> 1.87 us
    pallas_call x1, Pallas kernels: 42.7 us -> 31.7 us  [shards(): pl.pallas_call(functools.partial(kernel, (n_parts, n_dp, n_mp, chunk)), o...]
    reshape x1 -> x0, local copies, waits for them, and re-layouts: 1.29 us -> none  [shards(): gain.reshape(1, feats)]
where the time goes in v2:
time: 34.4 us; the launch traced here: 34.3 us
  Pallas kernels  31.7 us (92%)
  local copies, waits for them, and re-layouts  1.87 us (5%)
  between operations  0.66 us (2%)
    pallas_call x1, Pallas kernels, shards(): pl.pallas_call(functools.partial(kernel, (n_parts, n_dp, n_mp, chunk)), o...  31.7 us
    unnamed x1, local copies, waits for them, and re-layouts  1.87 us

profile of v2, /device:TPU:0, one launch (start us, length us, event | category | flops | bytes accessed | tf_op | source)
XLA Modules:
  0.0 34.3 jit_solution(10056875540480885236)
XLA Ops:
  0.7 31.7 %shard_map.82 = bf16[1024,256]{1,0:T(8,128)(2,1)} custom-call(s32[8]{0:T(128)} %owner_ref.1, s32[1]{0:T(128)S(6)} %copy.10.count_ref, s32[4]{0:T(128)} %store_ref.1, bf16[1024,2048]{1,0:T(8,128)(2,1)} %tok_hbm.1, bf16[2048]{0:T(1024)(128)(2,1)} %gain_ref.1, bf16[2048,1024]{1,0:T(8,128)(2,1)} %w_hbm.1, bf16[1,64,2048]{2,1,0:T(8,128)(2,1)} %bitcast.1, ...), custom_call_target="tpu_custom_call" | custom-call | tf_op jit(solution)/shard_map/pallas_call | solution.py:441
  32.4 1.9 %copy.11 = bf16[1024,256]{1,0:T(8,128)(2,1)} copy(bf16[1024,256]{1,0:T(8,128)(2,1)} %shard_map.82) | data formatting | bytes 1048576

commit v3 on v2

--- a/solution.py
+++ b/solution.py
@@ -9,6 +9,7 @@
 
 TILE = 128
 CORES = 2
+SUBS = 2
 MESH = pl.DeviceIdType.MESH
 F32 = jnp.float32
 BF16 = jnp.bfloat16
@@ -125,60 +126,62 @@
     own_rows = pl.ds(pl.multiple_of(me_z * rank, rank), rank)
     gath[own_rows, :feats] = down_ref[0]
     gath[own_rows, feats:] = up_ref[0]
-    piece = rank // n_parts
-
-    def part_of(a, p):
-        return gath.at[pl.ds(pl.multiple_of(a * rank + p * piece, 16), piece)]
-
-    def z_copy(a, to, sems):
-        ref = part_of(a, me_p)
+    piece = rank // n_parts // SUBS
+
+    def part_of(a, p, s):
+        return gath.at[pl.ds(pl.multiple_of(a * rank + (p * SUBS + s) * piece, 16), piece)]
+
+    def z_copy(a, to, sems, s):
+        ref = part_of(a, me_p, s)
         return pltpu.make_async_remote_copy(
-            ref, ref, sems.at[a], z_r.at[a], device_id={"dp": to}, device_id_type=MESH
-        )
-
-    def part_copy(a, k):
-        ref = part_of(a, me_p)
+            ref, ref, sems.at[a, s], z_r.at[a, s], device_id={"dp": to}, device_id_type=MESH
+        )
+
+    def part_copy(a, k, s):
+        ref = part_of(a, me_p, s)
         return pltpu.make_async_remote_copy(
             ref,
             ref,
-            part_s.at[a, k],
-            part_r.at[a, k],
+            part_s.at[a, k, s],
+            part_r.at[a, k, s],
             device_id={"parts": lax.rem(me_p + k, n_parts)},
             device_id_type=MESH,
         )
 
     @pl.when(has_up)
     def _():
-        z_copy(me_z, me_z + 1, up_s).start()
+        for s in range(SUBS):
+            z_copy(me_z, me_z + 1, up_s, s).start()
 
     @pl.when(has_dn)
     def _():
-        z_copy(me_z, me_z - 1, dn_s).start()
-
-    def relay(k):
+        for s in range(SUBS):
+            z_copy(me_z, me_z - 1, dn_s, s).start()
+
+    def relay(k, s):
         below, above = me_z - k, me_z + k
 
         @pl.when(below >= 0)
         def _():
-            z_copy(below, me_z, up_s).wait_recv()
+            z_copy(below, me_z, up_s, s).wait_recv()
 
             @pl.when(has_up)
             def _():
-                z_copy(below, me_z + 1, up_s).start()
+                z_copy(below, me_z + 1, up_s, s).start()
 
             for q in range(1, n_parts):
-                part_copy(below, q).start()
+                part_copy(below, q, s).start()
 
         @pl.when(above < n_dp)
         def _():
-            z_copy(above, me_z, dn_s).wait_recv()
+            z_copy(above, me_z, dn_s, s).wait_recv()
 
             @pl.when(has_dn)
             def _():
-                z_copy(above, me_z - 1, dn_s).start()
+                z_copy(above, me_z - 1, dn_s, s).start()
 
             for q in range(1, n_parts):
-                part_copy(above, q).start()
+                part_copy(above, q, s).start()
 
     def pair_copy(d, i):
         at = pl.ds(pl.multiple_of(i * chunk, chunk), chunk)
@@ -226,9 +229,14 @@
     for n, d in enumerate(order[:-1]):
         for i in range(chunks):
             base_step(n, d, i)
+            if n == 0 and i == chunks // 2 - 1:
+                relay(1, 0)
             if n == 0 and i == chunks // 2:
-                relay(1)
+                relay(1, 1)
         forward(d, chunks - 1)
+
+    if n_dp > 2:
+        relay(2, 0)
 
     ones = jnp.ones((feats, TILE), BF16)
     for i in range(chunks):
@@ -239,12 +247,16 @@
     for k in range(1, n_mp):
         sq_copy(sq, sq_s, sq_r, me, n_mp, k).start()
     if n_dp > 2:
-        relay(2)
+        relay(2, 1)
     for i in range(chunks):
         base_step(xs - 1, 0, i)
-        if i == chunks // 2 - 1:
-            for k in range(3, n_dp):
-                relay(k)
+        if n_dp > 3 and i == chunks // 2 - 2:
+            relay(3, 0)
+        if n_dp > 3 and i == chunks // 2 - 1:
+            relay(3, 1)
+            for k in range(4, n_dp):
+                for s in range(SUBS):
+                    relay(k, s)
 
     for a in range(n_dp):
 
@@ -252,15 +264,16 @@
         def _(a=a):
             for q in range(1, n_parts):
                 other = lax.rem(me_p + n_parts - q, n_parts)
-                ref = part_of(a, other)
-                pltpu.make_async_remote_copy(
-                    ref,
-                    ref,
-                    part_s.at[a, q],
-                    part_r.at[a, q],
-                    device_id={"parts": lax.rem(me_p + q, n_parts)},
-                    device_id_type=MESH,
-                ).wait_recv()
+                for s in range(SUBS):
+                    ref = part_of(a, other, s)
+                    pltpu.make_async_remote_copy(
+                        ref,
+                        ref,
+                        part_s.at[a, q, s],
+                        part_r.at[a, q, s],
+                        device_id={"parts": lax.rem(me_p + q, n_parts)},
+                        device_id_type=MESH,
+                    ).wait_recv()
 
     lane = lax.broadcasted_iota(jnp.int32, (TILE, lanes), 1)
     upper = lane >= rank
@@ -399,16 +412,19 @@
 
         @pl.when(jnp.logical_and(has_up, a <= me_z))
         def _(a=a):
-            z_copy(a, me_z, up_s).wait_send()
+            for s in range(SUBS):
+                z_copy(a, me_z, up_s, s).wait_send()
 
         @pl.when(jnp.logical_and(has_dn, a >= me_z))
         def _(a=a):
-            z_copy(a, me_z, dn_s).wait_send()
+            for s in range(SUBS):
+                z_copy(a, me_z, dn_s, s).wait_send()
 
         @pl.when(me_z != a)
         def _(a=a):
             for q in range(1, n_parts):
-                part_copy(a, q).wait_send()
+                for s in range(SUBS):
+                    part_copy(a, q, s).wait_send()
 
 
 def sq_copy(sq, sq_s, sq_r, me, n_mp, k):
@@ -469,11 +485,11 @@
             dma((far, chunks)),
             dma((n_mp,)),
             dma((n_mp,)),
-            dma((n_dp,)),
-            dma((n_dp,)),
-            dma((n_dp,)),
-            dma((n_dp, n_parts)),
-            dma((n_dp, n_parts)),
+            dma((n_dp, SUBS)),
+            dma((n_dp, SUBS)),
+            dma((n_dp, SUBS)),
+            dma((n_dp, n_parts, SUBS)),
+            dma((n_dp, n_parts, SUBS)),
             dma((2,)),
             dma((2,)),
             dma((far,)),

time: 34.4 us -> 33.6 us (0.977)
  Pallas kernels: 31.7 us -> 30.9 us
    pallas_call x1, Pallas kernels: 31.7 us -> 30.9 us  [shards(): pl.pallas_call(functools.partial(kernel, (n_parts, n_dp, n_mp, chunk)), o...]
where the time goes in v3:
time: 33.6 us; the launch traced here: 33.4 us
  Pallas kernels  30.9 us (92%)
  local copies, waits for them, and re-layouts  1.87 us (6%)
  between operations  0.66 us (2%)
    pallas_call x1, Pallas kernels, shards(): pl.pallas_call(functools.partial(kernel, (n_parts, n_dp, n_mp, chunk)), o...  30.9 us
    unnamed x1, local copies, waits for them, and re-layouts  1.87 us

profile of v3, /device:TPU:0, one launch (start us, length us, event | category | flops | bytes accessed | tf_op | source)
XLA Modules:
  0.0 33.4 jit_solution(376333283509098853)
XLA Ops:
  0.7 30.9 %shard_map.82 = bf16[1024,256]{1,0:T(8,128)(2,1)} custom-call(s32[8]{0:T(128)} %owner_ref.1, s32[1]{0:T(128)S(6)} %copy.10.count_ref, s32[4]{0:T(128)} %store_ref.1, bf16[1024,2048]{1,0:T(8,128)(2,1)} %tok_hbm.1, bf16[2048]{0:T(1024)(128)(2,1)} %gain_ref.1, bf16[2048,1024]{1,0:T(8,128)(2,1)} %w_hbm.1, bf16[1,64,2048]{2,1,0:T(8,128)(2,1)} %bitcast.1, ...), custom_call_target="tpu_custom_call" | custom-call | tf_op jit(solution)/shard_map/pallas_call | solution.py:457
  31.6 1.9 %copy.11 = bf16[1024,256]{1,0:T(8,128)(2,1)} copy(bf16[1024,256]{1,0:T(8,128)(2,1)} %shard_map.82) | data formatting | bytes 1048576

commit v4 on v3

--- a/solution.py
+++ b/solution.py
@@ -336,7 +336,11 @@
     for i in range(chunks):
         at = pl.ds(i * chunk, chunk)
         pair_copy(0, i).wait_recv()
-        acc[0, at] = acc[0, at] + pair_in[0, at].astype(F32)
+        value = acc[0, at] + pair_in[0, at].astype(F32)
+        for d in range(1, xs):
+            far_copy(d, i).wait_recv()
+            value = value + far_in[d - 1, at].astype(F32)
+        acc[0, at] = value
     total = sq[0]
     for k in range(1, n_mp):
         sq_copy(sq, sq_s, sq_r, me, n_mp, k).wait_recv()
@@ -384,18 +388,9 @@
             axis=1,
         ).astype(BF16)
         delta = jnp.dot(spread, gath[:, feats:], preferred_element_type=F32)
-        acc[0, at] = acc[0, at] + 2.0 * delta
-
-    for i in range(chunks):
-        for d in range(1, xs):
-            far_copy(d, i).wait_recv()
-        for t in range(i * chunk // TILE, (i + 1) * chunk // TILE):
-            at = slice(t * TILE, (t + 1) * TILE)
-            value = acc[0, at]
-            for d in range(1, xs):
-                value = value + far_in[d - 1, at].astype(F32)
-            scale = jnp.concatenate([sq_cols[at, :]] * (block // TILE), axis=1)
-            out_ref[at, :] = jnp.where(t < count_ref[0], value * scale, 0.0).astype(BF16)
+        scale = jnp.concatenate([sq_cols[at, :]] * (block // TILE), axis=1)
+        value = (acc[0, at] + 2.0 * delta) * scale
+        out_ref[at, :] = jnp.where(t < count_ref[0], value, 0.0).astype(BF16)
 
     for d in order:
         for i in range(chunks):

time: 33.6 us -> 33.5 us (level)
  no operation moved by 1% of the time
where the time goes in v4:
time: 33.5 us; the launch traced here: 33.3 us
  Pallas kernels  30.7 us (92%)
  local copies, waits for them, and re-layouts  1.87 us (6%)
  between operations  0.66 us (2%)
    pallas_call x1, Pallas kernels, shards(): pl.pallas_call(functools.partial(kernel, (n_parts, n_dp, n_mp, chunk)), o...  30.7 us
    unnamed x1, local copies, waits for them, and re-layouts  1.87 us

profile of v4, /device:TPU:0, one launch (start us, length us, event | category | flops | bytes accessed | tf_op | source)
XLA Modules:
  0.0 33.3 jit_solution(9437798837766616786)
XLA Ops:
  0.7 30.7 %shard_map.82 = bf16[1024,256]{1,0:T(8,128)(2,1)} custom-call(s32[8]{0:T(128)} %owner_ref.1, s32[1]{0:T(128)S(6)} %copy.10.count_ref, s32[4]{0:T(128)} %store_ref.1, bf16[1024,2048]{1,0:T(8,128)(2,1)} %tok_hbm.1, bf16[2048]{0:T(1024)(128)(2,1)} %gain_ref.1, bf16[2048,1024]{1,0:T(8,128)(2,1)} %w_hbm.1, bf16[1,64,2048]{2,1,0:T(8,128)(2,1)} %bitcast.1, ...), custom_call_target="tpu_custom_call" | custom-call | tf_op jit(solution)/shard_map/pallas_call | solution.py:452
  31.4 1.9 %copy.11 = bf16[1024,256]{1,0:T(8,128)(2,1)} copy(bf16[1024,256]{1,0:T(8,128)(2,1)} %shard_map.82) | data formatting | bytes 1048576
